TPU v7x, 32 devices: a whole 2x2x4 slice. The times are simulated.
32 devices in a mesh: group: 2 (over y), expert: 4 (over z), tensor: 2 (over x), dp: 2 (over core).
Axes of the slice: x: 2, y: 2, z: 4, core: 2. Of those that a mesh axis runs over, the one named last changes fastest.
Arguments:
- tokens: bfloat16 [2048, 3584], P(('group', 'expert', 'dp')), parts along dimension 0, may hold values from -6 to 6
- norm_gain: float32 [3584], replicated, may hold values from 0.25 to 1.75
- routes: int32 [2048, 2], P(('group', 'expert', 'dp')), parts along dimension 0, may hold values from 0 to 3, all different within a row; in each aligned block of 128 rows (0 to 127, 128 to 255, ...) at most 80 rows name the same one
- gate_values: bfloat16 [2048, 2], P(('group', 'expert', 'dp')), parts along dimension 0, may hold values from 0.19921875 to 1
- dense_gate: bfloat16 [2432, 3584], P(('tensor', 'dp'), 'expert'), may hold values from -0.09375 to 0.09375
- dense_up: bfloat16 [2432, 3584], P(('tensor', 'dp'), 'expert'), may hold values from -0.09375 to 0.09375
- dense_down: bfloat16 [2432, 3584], P(('tensor', 'dp'), 'expert'), may hold values from -0.125 to 0.125
- expert_gate: bfloat16 [4, 2432, 3584], P('expert', ('tensor', 'dp')), may hold values from -0.09375 to 0.09375
- expert_up: bfloat16 [4, 2432, 3584], P('expert', ('tensor', 'dp')), may hold values from -0.09375 to 0.09375
- expert_down: bfloat16 [4, 2432, 3584], P('expert', ('tensor', 'dp')), may hold values from -0.125 to 0.125
Outputs:
- mixed: bfloat16 [2048, 3584], P(('group', 'expert', 'dp'), 'tensor'), parts along dimension 0
There are 2 independent parts, one for each index of `group`. A program takes and returns all parts, laid end to end along the dimension named above; an argument that names none is the same for every part. Nothing has to cross between parts.
Inputs may be any that keep to these rules, and one draw needn't show every extreme that they name: `routes`: in each aligned block of 128 rows no expert is named by more than 80 of the ids, a bound that some block reaches; the 2 ids of a row differ.
All inputs are finite; a program needn't handle non-finite values.
Results may differ from a plain program's by a relative error of at most 0.0095.
Values may be sent and summed in bfloat16 or wider, within the bound.
A program may use at most 128 MiB of HBM per device.

v0:
```python
import jax
import jax.numpy as jnp
from jax import lax
from jax.sharding import PartitionSpec as P

EPSILON = 1e-05


def root_normed(tokens, norm_gain):
    values = tokens.astype(jnp.float32)
    route_scale_factor = lax.rsqrt(jnp.mean(values * values, axis=-1, keepdims=True) + EPSILON)
    return (values * route_scale_factor * norm_gain).astype(jnp.bfloat16)


def swiglu_rows(inputs, w_gate, w_up):
    dims = (((1,), (1,)), ((), ()))
    gate_part = lax.dot_general(inputs, w_gate, dims, preferred_element_type=jnp.float32)
    up_part = lax.dot_general(inputs, w_up, dims, preferred_element_type=jnp.float32)
    return (jax.nn.silu(gate_part) * up_part).astype(jnp.bfloat16)


def slot_tables(routes, gate_values, experts, capacity):
    blocks, tok_rows, picks = routes.shape
    pair_ids = routes.reshape(blocks, tok_rows * picks)
    expert_ids = jnp.arange(experts, dtype=jnp.int32)
    onehot = (pair_ids[:, :, None] == expert_ids[None, None, :]).astype(jnp.int32)
    before = jnp.cumsum(onehot, axis=1) - onehot
    position = jnp.sum(before * onehot, axis=2)
    slot_ids = jnp.arange(capacity, dtype=jnp.int32)
    slot_hits = onehot[:, :, :, None] * (
        position[:, :, None, None] == slot_ids[None, None, None, :]
    ).astype(jnp.int32)
    slot_hits = slot_hits.reshape(blocks, tok_rows, picks, experts, capacity).astype(jnp.float32)
    weights = gate_values.astype(jnp.float32)[:, :, :, None, None]
    placed = jnp.sum(slot_hits, axis=2).astype(jnp.bfloat16)
    gated = jnp.sum(slot_hits * weights, axis=2).astype(jnp.bfloat16)
    return (placed, gated)


def expert_apply(arrived, w_gate, w_up, w_down):
    slot_rows = arrived.reshape(-1, arrived.shape[-1])
    expert_hidden = swiglu_rows(slot_rows, w_gate, w_up)
    partial_value = jnp.dot(expert_hidden, w_down, preferred_element_type=jnp.float32)
    return partial_value.astype(jnp.bfloat16).reshape(arrived.shape)


def local(
    tokens,
    norm_gain,
    routes,
    gate_values,
    dense_gate,
    dense_up,
    dense_down,
    expert_gate,
    expert_up,
    expert_down,
):
    pairs = lax.axis_size("dp")
    tensors = lax.axis_size("tensor")
    experts = lax.axis_size("expert")
    tok_rows = tokens.shape[0]
    features = tokens.shape[1]
    capacity = 5 * tok_rows // (2 * experts)
    normed = root_normed(tokens, norm_gain)
    complete_gate_weight, full_up, full_down = (
        lax.all_gather(dense_gate, "expert", axis=1, tiled=True),
        lax.all_gather(dense_up, "expert", axis=1, tiled=True),
        lax.all_gather(dense_down, "expert", axis=1, tiled=True),
    )
    placed_own, unused_gates = slot_tables(routes[None], gate_values[None], experts, capacity)
    outgoing = jnp.einsum(
        "mrec,mrd->mecd", placed_own, normed[None], preferred_element_type=jnp.float32
    ).astype(jnp.bfloat16)
    incoming_rows = lax.all_to_all(outgoing, "expert", split_axis=1, concat_axis=1, tiled=True)
    group_rows, group_routes, grouped_gate_values, arrived = (
        lax.all_gather(normed, "dp", axis=0, tiled=True),
        lax.all_gather(routes, "dp", axis=0, tiled=True),
        lax.all_gather(gate_values, "dp", axis=0, tiled=True),
        lax.all_gather(incoming_rows, "dp", axis=0, tiled=True),
    )
    placed, gated = slot_tables(
        group_routes.reshape(pairs, tok_rows, -1),
        grouped_gate_values.reshape(pairs, tok_rows, -1),
        experts,
        capacity,
    )
    partial_value = expert_apply(arrived, expert_gate[0], expert_up[0], expert_down[0])
    returned = lax.all_to_all(partial_value, "expert", split_axis=1, concat_axis=1, tiled=True)
    expert_part = jnp.einsum("mrec,mecd->mrd", gated, returned, preferred_element_type=jnp.float32)
    dense_hidden = swiglu_rows(group_rows, complete_gate_weight, full_up)
    dense_part = jnp.dot(dense_hidden, full_down, preferred_element_type=jnp.float32)
    combined = dense_part + expert_part.reshape(dense_part.shape)
    width = features // tensors
    arranged = (
        combined.reshape(pairs, tok_rows, tensors, width)
        .transpose(2, 0, 1, 3)
        .reshape(tensors * pairs * tok_rows, width)
    )
    summed = lax.psum_scatter(
        arranged.astype(jnp.bfloat16), ("tensor", "dp"), scatter_dimension=0, tiled=True
    ).astype(jnp.float32)
    residual = lax.dynamic_slice_in_dim(tokens, lax.axis_index("tensor") * width, width, 1)
    return (residual.astype(jnp.float32) + summed).astype(jnp.bfloat16)


def solution(mesh):
    placed = (
        P(("group", "expert", "dp"), None),
        P(),
        P(("group", "expert", "dp"), None),
        P(("group", "expert", "dp"), None),
        P(("tensor", "dp"), "expert"),
        P(("tensor", "dp"), "expert"),
        P(("tensor", "dp"), "expert"),
        P("expert", ("tensor", "dp"), None),
        P("expert", ("tensor", "dp"), None),
        P("expert", ("tensor", "dp"), None),
    )
    return jax.shard_map(
        local,
        mesh=mesh,
        in_specs=placed,
        out_specs=P(("group", "expert", "dp"), "tensor"),
        check_vma=False,
    )
```

profile of v0, /device:TPU:0, one launch (start us, length us, event | category | flops | bytes accessed | tf_op | source)
XLA Modules:
  0.0 488.1 jit_solution(13655299658577651454)
XLA Ops:
  6.5 0.8 copy.52
  7.5 1.2 reduce-window.16
  8.8 0.7 fusion.26
  10.1 1.4 fusion.9
  11.6 1.5 fusion.11
  13.1 0.7 fusion.1
  13.8 58.6 %all_to_all.10 = bf16[1,4,80,3584]{3,2,0,1:T(8,128)(2,1)} all-to-all(bf16[1,4,80,3584]{3,2,0,1:T(8,128)(2,1)S(1)} %fusion.1), channel_id=1, replica_groups=mesh['group'=2,'expert'=4,'tensor'=2,'dp'=2] {'expert'}, dimensions={1} | all-to-all | bytes 4587520 | tf_op jit(solution)/shard_map/all_to_all | solution.py:75
  72.5 0.7 all-gather.6.cloned.1.call-update
  73.3 0.7 all-gather.8.cloned.1.call-update
  74.0 0.5 all-gather.10.cloned.1.call-update
  74.5 11.6 %all-gather.14.cloned.1.call-done = bf16[2,4,80,3584]{3,2,1,0:T(8,128)(2,1)} async-done(((bf16[1,4,80,3584]{3,2,1,0:T(8,128)(2,1)}), bf16[2,4,80,3584]{3,2,1,0:T(8,128)(2,1)}) %all-gather.14.cloned.1.call-update) | async-done | bytes 4587536 | tf_op jit(solution)/shard_map/all_gather | solution.py:80
  86.1 6.9 %fusion.7 = f32[640,608]{0,1:T(8,128)S(1)} fusion(bf16[640,3584]{1,0:T(8,128)(2,1)} %bitcast.63, bf16[1,608,3584]{2,1,0:T(8,128)(2,1)} %param.17), kind=kOutput, calls=%fused_computation.10 | convolution fusion | flops 2789212160 | bytes 10502144 | tf_op jit(solution)/shard_map/dot_general | solution.py:17
  93.1 3.6 multiply_convert_fusion
  96.7 4.0 convolution_convert_fusion
  100.7 2.4 copy.58
  103.1 5.0 %all-to-all-start.1 = ((bf16[2,4,80,3584]{3,2,0,1:T(8,128)(2,1)}), bf16[2,4,80,3584]{3,2,0,1:T(8,128)(2,1)}, u32[]{:S(2)}, u32[]{:S(2)}) async-start(bf16[2,4,80,3584]{3,2,0,1:T(8,128)(2,1)} %copy.58), calls=%async_computation.1 | async-start | bytes 9175040 | tf_op jit(solution)/shard_map/all_to_all | solution.py:89
  108.2 0.5 all-gather.12.cloned.1.call-update
  108.8 1.8 all_gather.25
  110.8 0.1 eq.122
  111.1 2.4 reduce-window.14
  114.2 1.9 all_gather.26
  116.3 151.4 %all-gather.8.cloned.1.call-done = bf16[608,3584]{1,0:T(8,128)(2,1)} async-done(((bf16[608,896]{1,0:T(8,128)(2,1)}), bf16[608,3584]{1,0:T(8,128)(2,1)}) %all-gather.8.cloned.1.call-update) | async-done | bytes 4358160 | tf_op jit(solution)/shard_map/all_gather | solution.py:67
  267.7 4.1 fusion.28
  271.8 8.8 %all-to-all-done.1 = bf16[2,4,80,3584]{3,2,0,1:T(8,128)(2,1)} async-done(((bf16[2,4,80,3584]{3,2,0,1:T(8,128)(2,1)}), bf16[2,4,80,3584]{3,2,0,1:T(8,128)(2,1)}, u32[]{:S(2)}, u32[]{:S(2)}) %all-to-all-start.1) | async-done | bytes 4587552 | tf_op jit(solution)/shard_map/all_to_all | solution.py:89
  280.7 5.2 %fusion.2 = f32[2,128,3584,1]{2,1,3,0:T(8,128)} fusion(bf16[2,4,80,3584]{3,2,0,1:T(8,128)(2,1)} %all-to-all-done.1, bf16[2,128,4,80]{1,3,2,0:T(8,128)(2,1)S(1)} %multiply_reduce_fusion), kind=kOutput, calls=%fused_computation.5 | convolution fusion | flops 587202560 | bytes 8421376 | tf_op jit(solution)/shard_map/mrec,mecd->mrd/dot_general | solution.py:90
  285.9 66.9 %all-gather.10.cloned.1.call-done = bf16[608,3584]{1,0:T(8,128)(2,1)} async-done(((bf16[608,896]{1,0:T(8,128)(2,1)}), bf16[608,3584]{1,0:T(8,128)(2,1)}) %all-gather.10.cloned.1.call-update) | async-done | bytes 4358160 | tf_op jit(solution)/shard_map/all_gather | solution.py:68
  352.8 83.4 %all-gather.12.cloned.1.call-done = bf16[608,3584]{1,0:T(8,128)(2,1)} async-done(((bf16[608,896]{1,0:T(8,128)(2,1)}), bf16[608,3584]{1,0:T(8,128)(2,1)}) %all-gather.12.cloned.1.call-update) | async-done | bytes 4358160 | tf_op jit(solution)/shard_map/all_gather | solution.py:69
  436.2 10.2 %fusion = bf16[256,3584]{1,0:T(8,128)(2,1)S(1)} fusion(f32[256,3584]{1,0:T(8,128)} %bitcast.55, bf16[608,3584]{1,0:T(8,128)(2,1)} %all-gather.12.cloned.1.call-done, bf16[256,3584]{1,0:T(8,128)(2,1)} %all-gather.6.cloned.1.call-done, bf16[608,3584]{1,0:T(8,128)(2,1)} %all-gather.10.cloned.1.call-done, f32[256,608]{0,1:T(8,128)S(1)} %fusion.28), kind=kOutput, calls=%fused_computation.3 | convolution fusion | flops 2234138624 | bytes 16678912 | tf_op jit(solution)/shard_map/dot_general | solution.py:92
  446.5 1.5 convert_element_type.147
  447.9 2.9 copy.60
  450.9 28.5 %reduce-scatter.2.cloned.1.call-done = bf16[128,1792]{1,0:T(8,128)(2,1)} async-done(((bf16[512,1792]{1,0:T(8,128)(2,1)}), bf16[128,1792]{1,0:T(8,128)(2,1)}) %reduce-scatter.2.cloned.1.call-update) | async-done | bytes 458768 | tf_op jit(solution)/shard_map/reduce_scatter | solution.py:100
  479.4 1.9 add_convert_fusion
  (63 shorter events, 2.2 us)
Async XLA Ops:
  6.5 79.6 %all-gather.14.cloned.1.call-start = ((), (), s32[]{:S(2)}) async-start(), calls=%async_computation.7 | async-start | bytes 6881280 | tf_op jit(solution)/shard_map/all_gather | solution.py:80
  13.1 59.4 %copy-start = (bf16[128,3584]{1,0:T(8,128)(2,1)}, bf16[128,3584]{1,0:T(8,128)(2,1)S(1)}, u32[]{:S(2)}) copy-start(bf16[128,3584]{1,0:T(8,128)(2,1)S(1)} %fusion.11) | copy-start | bytes 2752516
  72.5 43.8 %all-gather.6.cloned.1.call-start = ((), (), s32[]{:S(2)}) async-start(), calls=%async_computation.3 | async-start | bytes 2752512 | tf_op jit(solution)/shard_map/all_gather | solution.py:77
  73.2 194.5 %all-gather.8.cloned.1.call-start = ((), (), s32[]{:S(2)}) async-start(), calls=%async_computation.4 | async-start | bytes 5447680 | tf_op jit(solution)/shard_map/all_gather | solution.py:67
  74.0 278.8 %all-gather.10.cloned.1.call-start = ((), (), s32[]{:S(2)}) async-start(), calls=%async_computation.5 | async-start | bytes 5447680 | tf_op jit(solution)/shard_map/all_gather | solution.py:68
  74.0 19.0 %slice-start = ((s8[4358144]{0:T(1024)(128)(4,1)}), s8[163840]{0:T(1024)(128)(4,1)S(1)}, s32[]{:S(2)}) async-start(s8[4358144]{0:T(1024)(128)(4,1)} %bitcast.65), calls=%async_computation.9 | async-start | bytes 327680
  86.1 6.9 %copy-start.3 = (bf16[2,4,80,3584]{3,2,1,0:T(8,128)(2,1)S(1)}, bf16[2,4,80,3584]{3,2,1,0:T(8,128)(2,1)}, u32[]{:S(2)}) copy-start(bf16[2,4,80,3584]{3,2,1,0:T(8,128)(2,1)} %all-gather.14.cloned.1.call-done) | copy-start | bytes 13762564
  86.1 6.9 %slice-start.1 = ((s8[4358144]{0:T(1024)(128)(4,1)}), s8[4194304]{0:T(1024)(128)(4,1)S(1)}, s32[]{:S(2)}) async-start(s8[4358144]{0:T(1024)(128)(4,1)} %bitcast.65), calls=%async_computation.10 | async-start | bytes 8388608
  86.1 10.6 %slice-start.2 = ((s8[4358144]{0:T(1024)(128)(4,1)}), s8[4194304]{0:T(1024)(128)(4,1)S(1)}, s32[]{:S(2)}) async-start(s8[4358144]{0:T(1024)(128)(4,1)} %bitcast.67), calls=%async_computation.11 | async-start | bytes 8388608
  93.0 3.6 slice-start.3
  103.1 5.7 %copy-start.2 = (s32[128,2]{0,1:T(2,128)S(1)}, s32[128,2]{0,1:T(2,128)}, u32[]{:S(2)}) copy-start(s32[128,2]{0,1:T(2,128)} %param.12) | copy-start | bytes 3076
  103.1 11.0 %copy-start.4 = (bf16[128,2]{0,1:T(2,128)(2,1)S(1)}, bf16[128,2]{0,1:T(2,128)(2,1)}, u32[]{:S(2)}) copy-start(bf16[128,2]{0,1:T(2,128)(2,1)} %param.13) | copy-start | bytes 1540
  103.1 177.5 %all-to-all-start.1 = ((bf16[2,4,80,3584]{3,2,0,1:T(8,128)(2,1)}), bf16[2,4,80,3584]{3,2,0,1:T(8,128)(2,1)}, u32[]{:S(2)}, u32[]{:S(2)}) async-start(bf16[2,4,80,3584]{3,2,0,1:T(8,128)(2,1)} %copy.58), calls=%async_computation.1 | async-start | bytes 9175040 | tf_op jit(solution)/shard_map/all_to_all | solution.py:89
  108.2 328.0 %all-gather.12.cloned.1.call-start = ((), (), s32[]{:S(2)}) async-start(), calls=%async_computation.6 | async-start | bytes 5447680 | tf_op jit(solution)/shard_map/all_gather | solution.py:69
  108.8 370.6 %reduce-scatter.2.cloned.1.call-start = ((), (), s32[]{:S(2)}) async-start(), calls=%async_computation.8 | async-start | bytes 2293760 | tf_op jit(solution)/shard_map/reduce_scatter | solution.py:100
  446.5 32.9 %copy-start.1 = (bf16[128,3584]{1,0:T(8,128)(2,1)S(1)}, bf16[128,3584]{1,0:T(8,128)(2,1)}, u32[]{:S(2)}) copy-start(bf16[128,3584]{1,0:T(8,128)(2,1)} %param.10) | copy-start | bytes 2752516
Sparse Core Ops, SparseCore 0:
  72.6 13.4 all-gather.13
  87.6 11.3 all-gather.5
  100.6 167.0 all-gather.7
  269.2 83.5 all-gather.9
  354.2 81.9 all-gather.11
  451.0 28.3 reduce-scatter.1
where the time goes:
time: 489 us; the launch traced here: 488 us
  waiting for transfers between devices  353 us (72%)
  blocking collectives  62.4 us (13%)
  matrix products  34.8 us (7%)
  between operations  13.7 us (3%)
  other arithmetic  9.53 us (2%)
  local copies, waits for them, and re-layouts  9.32 us (2%)
  starting transfers between devices  5.24 us (1%)
    all_gather x1, waiting for transfers between devices, local(): lax.all_gather(dense_gate, 'expert', axis=1, tiled=True)  151 us
    all_gather x1, waiting for transfers between devices, local(): lax.all_gather(dense_down, 'expert', axis=1, tiled=True)  83.4 us
    all_gather x1, waiting for transfers between devices, local(): lax.all_gather(dense_up, 'expert', axis=1, tiled=True)  66.9 us
    all_to_all x1, blocking collectives, local(): lax.all_to_all(outgoing, 'expert', split_axis=1, concat_axis=1, tiled=True)  58.6 us
    reduce_scatter x1, waiting for transfers between devices, local(): lax.psum_scatter(arranged.astype(jnp.bfloat16), ('tensor', 'dp'), scatter...  28.5 us
    all_gather x1, waiting for transfers between devices, local(): lax.all_gather(incoming_rows, 'dp', axis=0, tiled=True)  11.6 us
    dot_general x2, matrix products, swiglu_rows(): lax.dot_general(inputs, w_gate, dims, preferred_element_type=jnp.float32)  11 us
    dot_general x1, matrix products, local(): jnp.dot(dense_hidden, full_down, preferred_element_type=jnp.float32)  10.2 us
  transfers between devices with their start and end apart: 7, of which 6 were waited for; matrix products, arithmetic and copies ran while one was open for 6% of the time, Pallas kernels for 0%

commit v1 on v0

v1 whole, which is shorter than its diff:
```python
import jax
import jax.numpy as jnp
from jax import lax
from jax.sharding import PartitionSpec as P

EPSILON = 1e-05
ROWS = (((1,), (1,)), ((), ()))


def root_normed(tokens, norm_gain):
    values = tokens.astype(jnp.float32)
    scale = lax.rsqrt(jnp.mean(values * values, axis=-1, keepdims=True) + EPSILON)
    return (values * scale * norm_gain).astype(jnp.bfloat16)


def swiglu(inputs, w_gate, w_up):
    gate_part = lax.dot_general(inputs, w_gate, ROWS, preferred_element_type=jnp.float32)
    up_part = lax.dot_general(inputs, w_up, ROWS, preferred_element_type=jnp.float32)
    return jax.nn.silu(gate_part) * up_part


def local(
    tokens,
    norm_gain,
    routes,
    gate_values,
    dense_gate,
    dense_up,
    dense_down,
    expert_gate,
    expert_up,
    expert_down,
):
    tensors = lax.axis_size("tensor")
    experts = lax.axis_size("expert")
    pairs = lax.axis_size("dp")
    tok_rows, features = tokens.shape
    hidden = dense_gate.shape[0]
    share = -(-hidden // experts)
    width = features // tensors
    me = lax.axis_index("expert")

    stacked = jnp.stack([dense_gate, dense_up, dense_down])
    stacked = jnp.pad(stacked, ((0, 0), (0, share * experts - hidden), (0, 0)))
    stacked = stacked.reshape(3, experts, share, -1)
    moved = lax.all_to_all(stacked, "expert", split_axis=1, concat_axis=1, tiled=True)
    moved = moved.transpose(0, 2, 1, 3).reshape(3, share, features)

    normed = root_normed(tokens, norm_gain)
    own_gates = jnp.sum(
        jnp.where(
            routes[:, :, None] == jnp.arange(experts, dtype=jnp.int32),
            gate_values.astype(jnp.float32)[:, :, None],
            0.0,
        ),
        axis=1,
    ).astype(jnp.bfloat16)
    every = lax.all_gather(normed, "expert", axis=0, tiled=False)
    every = lax.all_gather(every, "dp", axis=1, tiled=False).reshape(-1, features)
    gates = lax.all_gather(own_gates, ("expert", "dp"), axis=0, tiled=True)
    gate = lax.dynamic_slice_in_dim(gates, me, 1, 1).astype(jnp.float32)

    expert_hidden = (swiglu(every, expert_gate[0], expert_up[0]) * gate).astype(jnp.bfloat16)
    dense_hidden = swiglu(every, moved[0], moved[1]).astype(jnp.bfloat16)
    combined = jnp.dot(expert_hidden, expert_down[0], preferred_element_type=jnp.float32)
    combined = combined + jnp.dot(dense_hidden, moved[2], preferred_element_type=jnp.float32)

    arranged = (
        combined.astype(jnp.bfloat16)
        .reshape(experts, pairs, tok_rows, tensors, width)
        .transpose(3, 1, 0, 2, 4)
        .reshape(tensors * pairs, experts * tok_rows, width)
    )
    summed = lax.psum_scatter(arranged, ("tensor", "dp"), scatter_dimension=0, tiled=True)[0]
    summed = lax.psum_scatter(summed, "expert", scatter_dimension=0, tiled=True).astype(jnp.float32)
    residual = lax.dynamic_slice_in_dim(tokens, lax.axis_index("tensor") * width, width, 1)
    return (residual.astype(jnp.float32) + summed).astype(jnp.bfloat16)


def solution(mesh):
    placed = (
        P(("group", "expert", "dp"), None),
        P(),
        P(("group", "expert", "dp"), None),
        P(("group", "expert", "dp"), None),
        P(("tensor", "dp"), "expert"),
        P(("tensor", "dp"), "expert"),
        P(("tensor", "dp"), "expert"),
        P("expert", ("tensor", "dp"), None),
        P("expert", ("tensor", "dp"), None),
        P("expert", ("tensor", "dp"), None),
    )
    return jax.shard_map(
        local,
        mesh=mesh,
        in_specs=placed,
        out_specs=P(("group", "expert", "dp"), "tensor"),
        check_vma=False,
    )
```

time: 489 us -> 356 us (0.73)
  waiting for transfers between devices: 353 us -> 198 us
  local copies, waits for them, and re-layouts: 9.32 us -> 24.7 us
  matrix products: 34.8 us -> 47.4 us
    all_gather x5 -> x2, waiting for transfers between devices: 313 us -> 74.9 us  [the longest x1 74.9 us: local(): every = lax.all_gather(normed, 'expert', axis=0, tiled=False)]
    reduce_scatter x1 -> x2, waiting for transfers between devices: 28.5 us -> 109 us  [the longest x1 67.6 us: local(): lax.psum_scatter(arranged, ('tensor', 'dp'), scatter_dimension=0, tiled=T...]
    all_to_all x1 -> x0, blocking collectives: 58.6 us -> none  [local(): lax.all_to_all(outgoing, 'expert', split_axis=1, concat_axis=1, tiled=True)]
    all_gather x2 -> x1, blocking collectives: 3.73 us -> 59.6 us  [local(): gates = lax.all_gather(own_gates, ('expert', 'dp'), axis=0, tiled=True)]
    reshape x1, local copies, waits for them, and re-layouts: 2.42 us -> 15.4 us  [local(): arranged = combined.astype(jnp.bfloat16).reshape(experts, pairs, tok_rows...]
    dot_general x7 -> x4, matrix products: 34.8 us -> 47.4 us  [the longest x1 19 us: local(): jnp.dot(expert_hidden, expert_down[0], preferred_element_type=jnp.float32)]
    transpose x0 -> x1, local copies, waits for them, and re-layouts: none -> 7.41 us  [local(): arranged = combined.astype(jnp.bfloat16).reshape(experts, pairs, tok_rows...]
    all_to_all x1, waiting for transfers between devices: 8.83 us -> 13.9 us  [local(): lax.all_to_all(stacked, 'expert', split_axis=1, concat_axis=1, tiled=True)]
  transfers between devices with their start and end apart: 7 -> 5, of which waited for: 6 -> 4; matrix products, arithmetic and copies ran while one was open for 6% -> 1% of each run, Pallas kernels for 0% -> 0%
where the time goes in v1:
time: 356 us; the launch traced here: 355 us
  waiting for transfers between devices  198 us (56%)
  blocking collectives  59.6 us (17%)
  matrix products  47.4 us (13%)
  local copies, waits for them, and re-layouts  24.7 us (7%)
  between operations  13.3 us (4%)
  other arithmetic  7.91 us (2%)
  starting transfers between devices  3.97 us (1%)
    all_gather x1, waiting for transfers between devices, local(): every = lax.all_gather(normed, 'expert', axis=0, tiled=False)  74.9 us
    reduce_scatter x1, waiting for transfers between devices, local(): lax.psum_scatter(arranged, ('tensor', 'dp'), scatter_dimension=0, tiled=T...  67.6 us
    all_gather x1, blocking collectives, local(): gates = lax.all_gather(own_gates, ('expert', 'dp'), axis=0, tiled=True)  59.6 us
    reduce_scatter x1, waiting for transfers between devices, local(): lax.psum_scatter(summed, 'expert', scatter_dimension=0, tiled=True)  41.7 us
    dot_general x1, matrix products, local(): jnp.dot(expert_hidden, expert_down[0], preferred_element_type=jnp.float32)  19 us
    reshape x1, local copies, waits for them, and re-layouts, local(): arranged = combined.astype(jnp.bfloat16).reshape(experts, pairs, tok_rows...  15.4 us
    dot_general x1, matrix products, local(): jnp.dot(dense_hidden, moved[2], preferred_element_type=jnp.float32)  14.4 us
    dot_general x2, matrix products, swiglu(): lax.dot_general(inputs, w_gate, ROWS, preferred_element_type=jnp.float32)  14 us
  transfers between devices with their start and end apart: 5, of which 4 were waited for; matrix products, arithmetic and copies ran while one was open for 1% of the time, Pallas kernels for 0%

profile of v1, /device:TPU:0, one launch (start us, length us, event | category | flops | bytes accessed | tf_op | source)
XLA Modules:
  0.0 355.0 jit_solution(8068108493039147873)
XLA Ops:
  6.5 1.4 fusion.6
  8.0 2.4 fusion.8
  10.4 0.0 all-gather.5.cloned.1.call-update
  10.4 0.0 all-gather.7.cloned.1.call-start
  10.5 74.9 %all-gather.5.cloned.1.call-done = bf16[512,3584]{1,0:T(8,128)(2,1)} async-done(((bf16[128,3584]{1,0:T(8,128)(2,1)}), bf16[512,3584]{1,0:T(8,128)(2,1)}) %all-gather.5.cloned.1.call-update) | async-done | bytes 3670032 | tf_op jit(solution)/shard_map/all_gather | solution.py:58
  85.4 0.0 all-gather.7.cloned.1.call-update
  85.4 2.1 pad_maximum_fusion
  87.6 3.8 %all-to-all-start = ((bf16[3,4,152,896]{3,2,0,1:T(8,128)(2,1)}), bf16[3,4,152,896]{3,2,0,1:T(8,128)(2,1)S(1)}, u32[]{:S(2)}, u32[]{:S(2)}) async-start(bf16[3,4,152,896]{3,2,0,1:T(8,128)(2,1)} %pad_maximum_fusion), calls=%async_computation | async-start | bytes 6537216 | tf_op jit(solution)/shard_map/all_to_all | solution.py:46
  91.4 0.0 reduce-scatter.3.cloned.1.call-start
  91.5 59.6 %all_gather.19 = bf16[1024,4]{0,1:T(4,128)(2,1)S(1)} all-gather(bf16[128,4]{0,1:T(4,128)(2,1)S(1)} %select_reduce_fusion), channel_id=1, replica_groups=mesh['group'=2,'expert'=4,'tensor'=2,'dp'=2] {'expert','dp'}, dimensions={0}, use_global_device_ids=true | all-gather | bytes 9216 | tf_op jit(solution)/shard_map/all_gather | solution.py:60
  151.2 13.9 %all-to-all-done = bf16[3,4,152,896]{3,2,0,1:T(8,128)(2,1)S(1)} async-done(((bf16[3,4,152,896]{3,2,0,1:T(8,128)(2,1)}), bf16[3,4,152,896]{3,2,0,1:T(8,128)(2,1)S(1)}, u32[]{:S(2)}, u32[]{:S(2)}) %all-to-all-start) | async-done | bytes 3268640 | tf_op jit(solution)/shard_map/all_to_all | solution.py:46
  165.0 0.3 fusion.18
  165.3 0.4 copy.26
  165.7 0.1 copy.30
  165.9 0.4 copy.28
  166.3 0.1 copy.32
  166.4 0.4 copy.27
  166.9 0.1 copy.31
  167.0 0.0 all-gather.7.cloned.1.call-done
  167.0 10.6 %fusion.4 = f32[1024,608]{0,1:T(8,128)} fusion(bf16[1024,3584]{1,0:T(8,128)(2,1)} %bitcast.39, bf16[1,608,3584]{2,1,0:T(8,128)(2,1)} %param.17), kind=kOutput, calls=%fused_computation.5 | convolution fusion | flops 4462739456 | bytes 14188544 | tf_op jit(solution)/shard_map/dot_general | solution.py:17
  177.6 0.0 copy-done
  177.6 3.4 fusion.19
  181.0 19.0 %fusion = f32[1024,3584]{1,0:T(8,128)} fusion(bf16[1,608,3584]{2,1,0:T(8,128)(2,1)} %param.19, f32[1024,608]{0,1:T(8,128)} %fusion.4, bf16[1024,3584]{1,0:T(8,128)(2,1)} %bitcast.40, bf16[1,608,3584]{2,1,0:T(8,128)(2,1)} %param.18, f32[1024]{0:T(1024)S(1)} %bitcast.57), kind=kOutput, calls=%fused_computation.1 | convolution fusion | flops 8929837056 | bytes 33230848 | tf_op jit(solution)/shard_map/dot_general | solution.py:65
  200.0 14.4 %add_convert_fusion = bf16[1024,3584]{1,0:T(8,128)(2,1)} fusion(f32[1024,3584]{1,0:T(8,128)} %fusion, bf16[152,3584]{1,0:T(8,128)(2,1)S(1)} %bitcast.46, bf16[1024,3584]{1,0:T(8,128)(2,1)} %bitcast.41, bf16[152,3584]{1,0:T(8,128)(2,1)S(1)} %bitcast.47, f32[1024,152]{0,1:T(8,128)S(1)} %copy-done.5), kind=kOutput, calls=%fused_computation | convolution fusion | flops 2239643648 | bytes 32161792 | tf_op jit(solution)/shard_map/dot_general | solution.py:66
  214.4 15.4 %reshape.35 = bf16[4,2,128,2,1792]{4,3,2,1,0:T(2,128)(2,1)} reshape(bf16[1024,3584]{1,0:T(8,128)(2,1)} %add_convert_fusion) | data formatting | bytes 14680064 | tf_op jit(solution)/shard_map/reshape | solution.py:70
  229.8 7.4 %copy.29 = bf16[2,2,4,128,1792]{4,3,2,1,0:T(8,128)(2,1)} copy(bf16[2,2,4,128,1792]{4,0,3,1,2:T(2,128)(2,1)} %bitcast.44) | data formatting | bytes 14680064 | tf_op jit(solution)/shard_map/transpose | solution.py:71
  237.2 0.0 reduce-scatter.3.cloned.1.call-update
  237.2 0.0 reduce-scatter.5.cloned.1.call-start
  237.3 67.6 %reduce-scatter.3.cloned.1.call-done = bf16[1,512,1792]{2,1,0:T(8,128)(2,1)} async-done(((bf16[4,512,1792]{2,1,0:T(8,128)(2,1)}), bf16[1,512,1792]{2,1,0:T(8,128)(2,1)}) %reduce-scatter.3.cloned.1.call-update) | async-done | bytes 1835024 | tf_op jit(solution)/shard_map/reduce_scatter | solution.py:74
  304.8 0.0 reduce-scatter.5.cloned.1.call-update
  304.9 41.7 %reduce-scatter.5.cloned.1.call-done = bf16[128,1792]{1,0:T(8,128)(2,1)} async-done(((bf16[512,1792]{1,0:T(8,128)(2,1)}), bf16[128,1792]{1,0:T(8,128)(2,1)}) %reduce-scatter.5.cloned.1.call-update) | async-done | bytes 458768 | tf_op jit(solution)/shard_map/reduce_scatter | solution.py:75
  346.6 1.9 add_convert_fusion.1
  (20 shorter events, 0.1 us)
Async XLA Ops:
  6.5 78.9 %all-gather.5.cloned.1.call-start = ((), (), s32[]{:S(2)}) async-start(), calls=%async_computation.5 | async-start | bytes 4587520 | tf_op jit(solution)/shard_map/all_gather | solution.py:58
  10.4 75.0 %copy-start.2 = (bf16[608,896]{1,0:T(8,128)(2,1)S(1)}, bf16[608,896]{1,0:T(8,128)(2,1)}, u32[]{:S(2)}) copy-start(bf16[608,896]{1,0:T(8,128)(2,1)} %param.16) | copy-start | bytes 3268612
  10.4 75.0 %copy-start.3 = (bf16[608,896]{1,0:T(8,128)(2,1)S(1)}, bf16[608,896]{1,0:T(8,128)(2,1)}, u32[]{:S(2)}) copy-start(bf16[608,896]{1,0:T(8,128)(2,1)} %param.15) | copy-start | bytes 3268612
  10.4 75.0 %copy-start.4 = (bf16[608,896]{1,0:T(8,128)(2,1)S(1)}, bf16[608,896]{1,0:T(8,128)(2,1)}, u32[]{:S(2)}) copy-start(bf16[608,896]{1,0:T(8,128)(2,1)} %param.14) | copy-start | bytes 3268612
  10.4 156.6 %all-gather.7.cloned.1.call-start = ((), (), s32[]{:S(2)}) async-start(), calls=%async_computation.6 | async-start | bytes 11010048 | tf_op jit(solution)/shard_map/all_gather | solution.py:59
  87.6 3.9 %copy-start.7 = (bf16[128,2]{0,1:T(2,128)(2,1)S(1)}, bf16[128,2]{0,1:T(2,128)(2,1)}, u32[]{:S(2)}) copy-start(bf16[128,2]{0,1:T(2,128)(2,1)} %param.13) | copy-start | bytes 1540
  87.6 3.9 %copy-start.6 = (s32[128,2]{0,1:T(2,128)S(1)}, s32[128,2]{0,1:T(2,128)}, u32[]{:S(2)}) copy-start(s32[128,2]{0,1:T(2,128)} %param.12) | copy-start | bytes 3076
  87.6 77.5 %all-to-all-start = ((bf16[3,4,152,896]{3,2,0,1:T(8,128)(2,1)}), bf16[3,4,152,896]{3,2,0,1:T(8,128)(2,1)S(1)}, u32[]{:S(2)}, u32[]{:S(2)}) async-start(bf16[3,4,152,896]{3,2,0,1:T(8,128)(2,1)} %pad_maximum_fusion), calls=%async_computation | async-start | bytes 6537216 | tf_op jit(solution)/shard_map/all_to_all | solution.py:46
  91.4 213.4 %reduce-scatter.3.cloned.1.call-start = ((), (), s32[]{:S(2)}) async-start(), calls=%async_computation.3 | async-start | bytes 9175040 | tf_op jit(solution)/shard_map/reduce_scatter | solution.py:74
  167.0 10.6 %copy-start = (bf16[4,256,3584]{2,1,0:T(8,128)(2,1)S(1)}, bf16[4,256,3584]{2,1,0:T(8,128)(2,1)}, u32[]{:S(2)}) copy-start(bf16[4,256,3584]{2,1,0:T(8,128)(2,1)} %all-gather.7.cloned.1.call-done) | copy-start | bytes 22020100
  181.0 19.0 %copy-start.5 = (f32[1024,152]{0,1:T(8,128)S(1)}, f32[1024,152]{0,1:T(8,128)}, u32[]{:S(2)}) copy-start(f32[1024,152]{0,1:T(8,128)} %fusion.19) | copy-start | bytes 1867780
  237.2 109.4 %copy-start.1 = (bf16[128,3584]{1,0:T(8,128)(2,1)S(1)}, bf16[128,3584]{1,0:T(8,128)(2,1)}, u32[]{:S(2)}) copy-start(bf16[128,3584]{1,0:T(8,128)(2,1)} %param.10) | copy-start | bytes 2752516
  237.2 109.4 %reduce-scatter.5.cloned.1.call-start = ((), (), s32[]{:S(2)}) async-start(), calls=%async_computation.4 | async-start | bytes 2293760 | tf_op jit(solution)/shard_map/reduce_scatter | solution.py:75
Sparse Core Ops, SparseCore 0:
  10.5 74.7 all-gather.4
  86.9 16.9 all-gather.6
  237.4 67.4 reduce-scatter.2
  307.1 39.4 reduce-scatter.4

commit v2 on v1

--- a/solution.py
+++ b/solution.py
@@ -1,6 +1,10 @@
+import functools
+
 import jax
 import jax.numpy as jnp
 from jax import lax
+from jax.experimental import pallas as pl
+from jax.experimental.pallas import tpu as pltpu
 from jax.sharding import PartitionSpec as P
 
 EPSILON = 1e-05
@@ -19,7 +23,7 @@
     return jax.nn.silu(gate_part) * up_part
 
 
-def local(
+def local_plain(
     tokens,
     norm_gain,
     routes,
@@ -77,6 +81,318 @@
     return (residual.astype(jnp.float32) + summed).astype(jnp.bfloat16)
 
 
+def meet(partners):
+    barrier = pltpu.get_barrier_semaphore()
+    for partner in partners:
+        pl.semaphore_signal(
+            barrier, inc=1, device_id=partner, device_id_type=pl.DeviceIdType.MESH
+        )
+    pl.semaphore_wait(barrier, len(partners))
+
+
+def spread_kernel(
+    experts, x_ref, g_ref, w_ref, every, gates, moved, loc, zs, zr, gs, gr, ws, wr, xs, xr, ds, dr, ys, yr
+):
+    group, me = lax.axis_index("group"), lax.axis_index("expert")
+    t, d = lax.axis_index("tensor"), lax.axis_index("dp")
+    width = x_ref.shape[1] // 2
+    part = w_ref.shape[1] // 2
+    beside = {"dp": 1 - d}
+    across = {"tensor": 1 - t}
+    twin = {"group": 1 - group}
+    peers = [lax.rem(me + k, experts) for k in range(1, experts)]
+    meet([{"expert": e} for e in peers] + [beside, across, twin])
+
+    mine = pl.ds(pl.multiple_of(t * width, 128), width)
+    theirs = pl.ds(pl.multiple_of((1 - t) * width, 128), width)
+    rows = pl.ds(pl.multiple_of(group * part, 16), part)
+
+    def send(src, dst, to, s, r):
+        return pltpu.make_async_remote_copy(
+            src_ref=src,
+            dst_ref=dst,
+            send_sem=s,
+            recv_sem=r,
+            device_id=to,
+            device_id_type=pl.DeviceIdType.MESH,
+        )
+
+    started = []
+    for k, e in enumerate(peers):
+        z = send(x_ref.at[:, mine], every.at[me, d, :, mine], {"expert": e}, zs.at[k], zr.at[k])
+        z.start()
+        started.append(z)
+        z = send(g_ref, gates.at[me, d], {"expert": e}, gs.at[k], gr.at[k])
+        z.start()
+        started.append(z)
+    weights = []
+    for k, e in enumerate(peers):
+        z = send(w_ref.at[e, rows], moved.at[me, rows], {"expert": e}, ws.at[k], wr.at[k])
+        z.start()
+        started.append(z)
+    n = experts - 1
+    own = send(x_ref, every.at[me, d], beside, ds.at[3 * n], dr.at[3 * n])
+    own.start()
+    own_gates = send(g_ref, gates.at[me, d], beside, ds.at[3 * n + 1], dr.at[3 * n + 1])
+    own_gates.start()
+    here = [
+        pltpu.make_async_copy(x_ref, every.at[me, d], loc.at[0]),
+        pltpu.make_async_copy(g_ref, gates.at[me, d], loc.at[1]),
+        pltpu.make_async_copy(w_ref.at[me], moved.at[me], loc.at[2]),
+    ]
+    for c in here:
+        c.start()
+
+    sources = [lax.rem(me + experts - k, experts) for k in range(1, experts)]
+    passed = []
+    for k, e in enumerate(sources):
+        block = every.at[e, d, :, mine]
+        send(block, block, {"expert": e}, zs.at[k], zr.at[k]).wait_recv()
+        c = send(block, block, across, xs.at[k], xr.at[k])
+        c.start()
+        passed.append(c)
+        c = send(block, block, beside, ds.at[k], dr.at[k])
+        c.start()
+        passed.append(c)
+        block = gates.at[e, d]
+        send(block, block, {"expert": e}, gs.at[k], gr.at[k]).wait_recv()
+        c = send(block, block, beside, ds.at[2 * n + k], dr.at[2 * n + k])
+        c.start()
+        passed.append(c)
+    for k, e in enumerate(sources):
+        block = moved.at[e, rows]
+        send(block, block, {"expert": e}, ws.at[k], wr.at[k]).wait_recv()
+        c = send(block, block, twin, ys.at[k], yr.at[k])
+        c.start()
+        passed.append(c)
+    for k, e in enumerate(sources):
+        block = every.at[e, d, :, theirs]
+        send(block, block, across, xs.at[k], xr.at[k]).wait_recv()
+        c = send(block, block, beside, ds.at[n + k], dr.at[n + k])
+        c.start()
+        started.append(c)
+    other = pl.ds(pl.multiple_of((1 - group) * part, 16), part)
+    for k, e in enumerate(sources):
+        block = every.at[e, 1 - d, :, mine]
+        send(block, block, beside, ds.at[k], dr.at[k]).wait_recv()
+        block = every.at[e, 1 - d, :, theirs]
+        send(block, block, beside, ds.at[n + k], dr.at[n + k]).wait_recv()
+        block = gates.at[e, 1 - d]
+        send(block, block, beside, ds.at[2 * n + k], dr.at[2 * n + k]).wait_recv()
+        block = moved.at[e, other]
+        send(block, block, twin, ys.at[k], yr.at[k]).wait_recv()
+    own.wait()
+    own_gates.wait()
+    for c in here:
+        c.wait()
+    for c in started + passed:
+        c.wait_send()
+
+
+def spread(experts, x, gates, weights):
+    n = experts - 1
+    dma = pltpu.SemaphoreType.DMA
+    anywhere = pl.BlockSpec(memory_space=pl.ANY)
+    return pl.pallas_call(
+        functools.partial(spread_kernel, experts),
+        out_shape=(
+            jax.ShapeDtypeStruct((experts, 2) + x.shape, x.dtype),
+            jax.ShapeDtypeStruct((experts, 2) + gates.shape, gates.dtype),
+            jax.ShapeDtypeStruct(weights.shape, weights.dtype),
+        ),
+        in_specs=[anywhere] * 3,
+        out_specs=(anywhere,) * 3,
+        scratch_shapes=[dma((3,))]
+        + [dma((n,))] * 8
+        + [dma((3 * n + 2,))] * 2
+        + [dma((n,))] * 2,
+        compiler_params=pltpu.CompilerParams(
+            collective_id=0, has_side_effects=True, vmem_limit_bytes=4 * 1024 * 1024
+        ),
+        cost_estimate=pl.CostEstimate(flops=0, bytes_accessed=30000000, transcendentals=0),
+    )(x, gates, weights)
+
+
+def layer_kernel(
+    experts, tok_ref, every, gates, moved, w_gate, w_up, w_down, out_ref,
+    outgoing, kept, from_beside, from_across, zsend, zrecv, ds, dr, xs, xr, zs, zr,
+):
+    me, t, d = lax.axis_index("expert"), lax.axis_index("tensor"), lax.axis_index("dp")
+    beside, across = {"dp": 1 - d}, {"tensor": 1 - t}
+    peers = [lax.rem(me + k, experts) for k in range(1, experts)]
+    meet([{"expert": e} for e in peers] + [beside, across])
+
+    tok_rows, features = tok_ref.shape
+    width = features // 2
+    cut = moved.shape[2]
+    share = moved.shape[1] // 3
+    per_half = width // cut
+    f32 = jnp.float32
+
+    def send(src, dst, to, s, r):
+        return pltpu.make_async_remote_copy(
+            src_ref=src,
+            dst_ref=dst,
+            send_sem=s,
+            recv_sem=r,
+            device_id=to,
+            device_id_type=pl.DeviceIdType.MESH,
+        )
+
+    def by_beside(j):
+        return send(outgoing.at[j], from_beside.at[j], beside, ds.at[j], dr.at[j])
+
+    def by_across(j):
+        return send(kept.at[j, 1 - t], from_across.at[j], across, xs.at[j], xr.at[j])
+
+    def by_expert(j):
+        return send(
+            zsend.at[j], zrecv.at[j], {"expert": lax.rem(me + 1 + j, experts)}, zs.at[j], zr.at[j]
+        )
+
+    def block_sums(e, b):
+        x = every[e, b]
+        lanes = gates[e, b].astype(f32)
+        column = lax.broadcasted_iota(jnp.int32, lanes.shape, 1)
+        gate = jnp.sum(jnp.where(column == me, lanes, 0.0), axis=1, keepdims=True)
+        g = lax.dot_general(x, w_gate[0], ROWS, preferred_element_type=f32)
+        u = lax.dot_general(x, w_up[0], ROWS, preferred_element_type=f32)
+        routed = (g / (1.0 + jnp.exp(-g)) * u * gate).astype(jnp.bfloat16)
+        both = jnp.zeros((tok_rows, 2 * share), f32)
+        for i in range(experts):
+            both += lax.dot_general(
+                x[:, i * cut : (i + 1) * cut],
+                moved[i, : 2 * share],
+                ROWS,
+                preferred_element_type=f32,
+            )
+        g, u = both[:, :share], both[:, share:]
+        dense = (g / (1.0 + jnp.exp(-g)) * u).astype(jnp.bfloat16)
+        sums = []
+        for i in range(experts):
+            s = jnp.dot(
+                routed, w_down[0, :, i * cut : (i + 1) * cut], preferred_element_type=f32
+            )
+            s += jnp.dot(dense, moved[i, 2 * share :], preferred_element_type=f32)
+            sums.append(s.astype(jnp.bfloat16))
+        return sums
+
+    def compute(j):
+        e = lax.rem(me + 1 + j, experts)
+        for dst, b in ((outgoing, 1 - d), (kept, d)):
+            for i, s in enumerate(block_sums(e, b)):
+                at = (i % per_half) * cut
+                dst[j, i // per_half, :, at : at + cut] = s
+            if dst is outgoing:
+                by_beside(j).start()
+
+    def join_pair(j):
+        by_beside(j).wait_recv()
+        kept[j] = (kept[j].astype(f32) + from_beside[j].astype(f32)).astype(jnp.bfloat16)
+        by_across(j).start()
+
+    def join_tensor(j):
+        by_across(j).wait_recv()
+        total = kept[j, t].astype(f32) + from_across[j].astype(f32)
+        zsend[j] = total.astype(jnp.bfloat16)
+
+    def turn(j, carry):
+        compute(j)
+
+        @pl.when(j >= 1)
+        def _():
+            join_pair(j - 1)
+
+        @pl.when(j >= 2)
+        def _():
+            join_tensor(j - 2)
+            by_expert(j - 2).start()
+
+        return carry
+
+    lax.fori_loop(0, experts, turn, 0)
+    last = experts - 1
+    join_pair(last)
+    join_tensor(last - 1)
+    by_expert(last - 1).start()
+    by_across(last).wait_recv()
+    own = pl.ds(pl.multiple_of(t * width, 128), width)
+    total = kept[last, t].astype(f32) + from_across[last].astype(f32)
+    total += tok_ref[:, own].astype(f32)
+    for j in range(last):
+        by_expert(j).wait_recv()
+        total += zrecv[j].astype(f32)
+    out_ref[...] = total.astype(out_ref.dtype)
+    for j in range(experts):
+        by_beside(j).wait_send()
+        by_across(j).wait_send()
+    for j in range(last):
+        by_expert(j).wait_send()
+
+
+def layer(experts, tokens, every, gates, moved, w_gate, w_up, w_down):
+    tok_rows, features = tokens.shape
+    width = features // 2
+    dma = pltpu.SemaphoreType.DMA
+    inside = pl.BlockSpec(memory_space=pltpu.VMEM)
+    kind = tokens.dtype
+    return pl.pallas_call(
+        functools.partial(layer_kernel, experts),
+        out_shape=jax.ShapeDtypeStruct((tok_rows, width), kind),
+        in_specs=[inside] * 7,
+        out_specs=inside,
+        scratch_shapes=[
+            pltpu.VMEM((experts, 2, tok_rows, width), kind),
+            pltpu.VMEM((experts, 2, tok_rows, width), kind),
+            pltpu.VMEM((experts, 2, tok_rows, width), kind),
+            pltpu.VMEM((experts, tok_rows, width), kind),
+            pltpu.VMEM((experts - 1, tok_rows, width), kind),
+            pltpu.VMEM((experts - 1, tok_rows, width), kind),
+        ]
+        + [dma((experts,))] * 4
+        + [dma((experts - 1,))] * 2,
+        compiler_params=pltpu.CompilerParams(
+            collective_id=1, has_side_effects=True, vmem_limit_bytes=56 * 1024 * 1024
+        ),
+        cost_estimate=pl.CostEstimate(
+            flops=17000000000, bytes_accessed=30000000, transcendentals=1000000
+        ),
+    )(tokens, every, gates, moved, w_gate, w_up, w_down)
+
+
+def local_kernels(
+    tokens,
+    norm_gain,
+    routes,
+    gate_values,
+    dense_gate,
+    dense_up,
+    dense_down,
+    expert_gate,
+    expert_up,
+    expert_down,
+):
+    experts = lax.axis_size("expert")
+    hidden, cut = dense_gate.shape
+    share = -(-hidden // (32 * experts)) * 32
+
+    weights = jnp.stack([dense_gate, dense_up, dense_down])
+    weights = jnp.pad(weights, ((0, 0), (0, share * experts - hidden), (0, 0)))
+    weights = weights.reshape(3, experts, share, cut).transpose(1, 0, 2, 3)
+    weights = weights.reshape(experts, 3 * share, cut)
+    normed = root_normed(tokens, norm_gain)
+    own_gates = jnp.sum(
+        jnp.where(
+            routes[:, :, None] == jnp.arange(128, dtype=jnp.int32),
+            gate_values.astype(jnp.float32)[:, :, None],
+            0.0,
+        ),
+        axis=1,
+    ).astype(jnp.bfloat16)
+    every, gates, moved = spread(experts, normed, own_gates, weights)
+    return layer(experts, tokens, every, gates, moved, expert_gate, expert_up, expert_down)
+
+
 def solution(mesh):
     placed = (
         P(("group", "expert", "dp"), None),
@@ -90,8 +406,10 @@
         P("expert", ("tensor", "dp"), None),
         P("expert", ("tensor", "dp"), None),
     )
+    sizes = dict(mesh.shape)
+    paired = sizes["group"] == 2 and sizes["tensor"] == 2 and sizes["dp"] == 2
     return jax.shard_map(
-        local,
+        local_kernels if paired else local_plain,
         mesh=mesh,
         in_specs=placed,
         out_specs=P(("group", "expert", "dp"), "tensor"),

time: 356 us -> 203 us (0.57)
  waiting for transfers between devices: 198 us -> 0 us
  Pallas kernels: 0 us -> 188 us
  blocking collectives: 59.6 us -> 0 us
  matrix products: 47.4 us -> 0 us
  local copies, waits for them, and re-layouts: 24.7 us -> 7.58 us
  between operations: 13.3 us -> 0.07 us
  starting transfers between devices: 3.97 us -> 0 us
    pallas_call x0 -> x2, Pallas kernels: none -> 188 us  [the longest x1 96.3 us: spread(): pl.pallas_call(functools.partial(spread_kernel, experts), out_shape=(jax....]
    reduce_scatter x2 -> x0, waiting for transfers between devices: 109 us -> none  [the longest x1 67.6 us: local(): lax.psum_scatter(arranged, ('tensor', 'dp'), scatter_dimension=0, tiled=T...]
    all_gather x2 -> x0, waiting for transfers between devices: 74.9 us -> none  [the longest x1 74.9 us: local(): every = lax.all_gather(normed, 'expert', axis=0, tiled=False)]
    all_gather x1 -> x0, blocking collectives: 59.6 us -> none  [local(): gates = lax.all_gather(own_gates, ('expert', 'dp'), axis=0, tiled=True)]
    dot_general x4 -> x0, matrix products: 47.4 us -> none  [the longest x1 19 us: local(): jnp.dot(expert_hidden, expert_down[0], preferred_element_type=jnp.float32)]
    reshape x1, local copies, waits for them, and re-layouts: 15.4 us -> 0.28 us  [local_kernels(): weights = weights.reshape(3, experts, share, cut).transpose(1, 0, 2, 3)]
    all_to_all x1 -> x0, waiting for transfers between devices: 13.9 us -> none  [local(): lax.all_to_all(stacked, 'expert', split_axis=1, concat_axis=1, tiled=True)]
    transpose x1 -> x0, local copies, waits for them, and re-layouts: 7.41 us -> none  [local(): arranged = combined.astype(jnp.bfloat16).reshape(experts, pairs, tok_rows...]
  transfers between devices with their start and end apart: 5 -> 0, of which waited for: 4 -> 0; matrix products, arithmetic and copies ran while one was open for 1% -> 0% of each run, Pallas kernels for 0% -> 0%
where the time goes in v2:
time: 203 us; the launch traced here: 202 us
  Pallas kernels  188 us (93%)
  local copies, waits for them, and re-layouts  7.58 us (4%)
  other arithmetic  7.05 us (3%)
    pallas_call x1, Pallas kernels, spread(): pl.pallas_call(functools.partial(spread_kernel, experts), out_shape=(jax....  96.3 us
    pallas_call x1, Pallas kernels, layer(): pl.pallas_call(functools.partial(layer_kernel, experts), out_shape=jax.Sh...  91.3 us
    unnamed x11, local copies, waits for them, and re-layouts  7.31 us

profile of v2, /device:TPU:0, one launch (start us, length us, event | category | flops | bytes accessed | tf_op | source)
XLA Modules:
  0.0 202.4 jit_solution(2047058456436631321)
XLA Ops:
  0.0 0.0 copy-start.3
  0.0 0.0 copy-start.4
  0.0 1.6 fusion.5
  1.6 0.7 convert_element_type.16
  2.3 0.8 select_reduce_fusion.g_ref
  3.1 1.5 fusion.7.x_ref
  4.6 0.0 copy-done.3
  4.6 0.0 copy-done.4
  4.6 2.5 %fusion.4 = bf16[3,640,896]{2,1,0:T(8,128)(2,1)S(1)} fusion(bf16[1,608,896]{2,1,0:T(8,128)(2,1)S(1)} %bitcast.9, bf16[1,608,896]{2,1,0:T(8,128)(2,1)S(1)} %bitcast.10, bf16[1,608,896]{2,1,0:T(8,128)(2,1)} %bitcast.11), kind=kLoop, calls=%fused_computation.5 | loop fusion | flops 17203200 | bytes 6709248 | tf_op jit(solution)/shard_map/stack | solution.py:379
  7.1 0.3 copy.14
  7.4 96.3 %shard_map.100 = (bf16[4,2,128,3584]{3,2,1,0:T(8,128)(2,1)S(1)}, bf16[4,2,128,128]{3,2,1,0:T(8,128)(2,1)S(1)}, bf16[4,480,896]{2,1,0:T(8,128)(2,1)S(1)}) custom-call(bf16[128,3584]{1,0:T(8,128)(2,1)S(1)} %fusion.7.x_ref, bf16[128,128]{1,0:T(8,128)(2,1)S(1)} %select_reduce_fusion.g_ref, bf16[4,480,896]{2,1,0:T(8,128)(2,1)S(1)} %bitcast.7), custom_call_target="tpu_custom_call" | custom-call | bytes 30000000 | tf_op jit(solution)/shard_map/pallas_call | solution.py:196
  103.7 0.0 copy-start
  103.7 3.0 %copy-done = bf16[4,2,128,3584]{3,2,1,0:T(8,128)(2,1)} copy-done((bf16[4,2,128,3584]{3,2,1,0:T(8,128)(2,1)}, bf16[4,2,128,3584]{3,2,1,0:T(8,128)(2,1)S(1)}, u32[]{:S(2)}) %copy-start) | copy-done | bytes 7340056
  106.7 0.0 copy-start.1
  106.7 1.8 copy-done.1
  108.5 0.0 copy-start.2
  108.5 0.7 copy-done.2
  109.2 91.3 %shard_map.101 = bf16[128,1792]{1,0:T(8,128)(2,1)} custom-call(bf16[128,3584]{1,0:T(8,128)(2,1)} %tok_ref.1, bf16[4,2,128,3584]{3,2,1,0:T(8,128)(2,1)} %copy-done, bf16[4,2,128,128]{3,2,1,0:T(8,128)(2,1)} %copy-done.2, bf16[4,480,896]{2,1,0:T(8,128)(2,1)} %copy-done.1, bf16[1,608,3584]{2,1,0:T(8,128)(2,1)} %w_gate.1, bf16[1,608,3584]{2,1,0:T(8,128)(2,1)} %w_up.1, ...), custom_call_target="tpu_custom_call" | custom-call | flops 16999999488 | bytes 30000000 | tf_op jit(solution)/shard_map/pallas_call | solution.py:339
  200.6 1.8 copy.16
  (1 shorter events, 0.0 us)
Async XLA Ops:
  0.0 4.6 %copy-start.3 = (bf16[608,896]{1,0:T(8,128)(2,1)S(1)}, bf16[608,896]{1,0:T(8,128)(2,1)}, u32[]{:S(2)}) copy-start(bf16[608,896]{1,0:T(8,128)(2,1)} %param.16) | copy-start | bytes 3268612
  0.0 4.6 %copy-start.4 = (bf16[608,896]{1,0:T(8,128)(2,1)S(1)}, bf16[608,896]{1,0:T(8,128)(2,1)}, u32[]{:S(2)}) copy-start(bf16[608,896]{1,0:T(8,128)(2,1)} %param.15) | copy-start | bytes 3268612
  103.7 3.0 %copy-start = (bf16[4,2,128,3584]{3,2,1,0:T(8,128)(2,1)}, bf16[4,2,128,3584]{3,2,1,0:T(8,128)(2,1)S(1)}, u32[]{:S(2)}) copy-start(bf16[4,2,128,3584]{3,2,1,0:T(8,128)(2,1)S(1)} %get-tuple-element.8.every) | copy-start | bytes 22020100
  106.7 1.8 copy-start.1
  108.5 0.7 copy-start.2

commit v3 on v1

--- a/solution.py
+++ b/solution.py
@@ -1,6 +1,10 @@
+import functools
+
 import jax
 import jax.numpy as jnp
 from jax import lax
+from jax.experimental import pallas as pl
+from jax.experimental.pallas import tpu as pltpu
 from jax.sharding import PartitionSpec as P
 
 EPSILON = 1e-05
@@ -19,7 +23,7 @@
     return jax.nn.silu(gate_part) * up_part
 
 
-def local(
+def local_plain(
     tokens,
     norm_gain,
     routes,
@@ -77,6 +81,299 @@
     return (residual.astype(jnp.float32) + summed).astype(jnp.bfloat16)
 
 
+def meet(partners):
+    barrier = pltpu.get_barrier_semaphore()
+    for partner in partners:
+        pl.semaphore_signal(
+            barrier, inc=1, device_id=partner, device_id_type=pl.DeviceIdType.MESH
+        )
+    pl.semaphore_wait(barrier, len(partners))
+
+
+def layer_kernel(
+    experts, tok_ref, x_ref, g_ref, w_ref, eg_ref, eu_ref, ed_ref, out_ref,
+    every, gates, moved, w_gate, w_up, w_down,
+    sums, from_beside, from_across, zsend, zrecv,
+    loc, tzs, tzr, gzs, gzr, wzs, wzr, wys, wyr, txs, txr, tds, tdr, os, orr,
+    ds, dr, xs, xr, zs, zr,
+):
+    group, me = lax.axis_index("group"), lax.axis_index("expert")
+    t, d = lax.axis_index("tensor"), lax.axis_index("dp")
+    beside, across, twin = {"dp": 1 - d}, {"tensor": 1 - t}, {"group": 1 - group}
+    meet([{"expert": lax.rem(me + k, experts)} for k in range(1, experts)] + [beside, across, twin])
+
+    tok_rows, features = tok_ref.shape
+    width = features // 2
+    cut = moved.shape[2]
+    share = moved.shape[1] // 3
+    part = moved.shape[1] // 2
+    per_half = width // cut
+    f32 = jnp.float32
+    mine = pl.ds(pl.multiple_of(t * width, 128), width)
+    theirs = pl.ds(pl.multiple_of((1 - t) * width, 128), width)
+    rows = pl.ds(pl.multiple_of(group * part, 16), part)
+    other_rows = pl.ds(pl.multiple_of((1 - group) * part, 16), part)
+
+    def send(src, dst, to, s, r):
+        return pltpu.make_async_remote_copy(
+            src_ref=src,
+            dst_ref=dst,
+            send_sem=s,
+            recv_sem=r,
+            device_id=to,
+            device_id_type=pl.DeviceIdType.MESH,
+        )
+
+    def source(j):
+        return lax.rem(me + experts - j, experts)
+
+    def target(j):
+        e = lax.rem(me + j, experts)
+        return e, {"expert": e}
+
+    def weight_send(j):
+        e, to = target(j)
+        return send(w_ref.at[e, rows], moved.at[me, rows], to, wzs.at[j], wzr.at[j])
+
+    def weight_twin(j, which):
+        block = moved.at[source(j), which]
+        return send(block, block, twin, wys.at[j], wyr.at[j])
+
+    def token_send(j):
+        e, to = target(j)
+        return send(x_ref.at[:, mine], every.at[me, d, :, mine], to, tzs.at[j], tzr.at[j])
+
+    def gate_send(j):
+        e, to = target(j)
+        return send(g_ref, gates.at[me, d], to, gzs.at[j], gzr.at[j])
+
+    def token_across(j, which):
+        block = every.at[source(j), d, :, which]
+        return send(block, block, across, txs.at[j], txr.at[j])
+
+    def token_beside(j, b, which, i):
+        block = every.at[source(j), b, :, which]
+        return send(block, block, beside, tds.at[i, j], tdr.at[i, j])
+
+    def gate_beside(j, b):
+        block = gates.at[source(j), b]
+        return send(block, block, beside, tds.at[2, j], tdr.at[2, j])
+
+    own = send(x_ref, every.at[me, d], beside, os.at[0], orr.at[0])
+    own_gates = send(g_ref, gates.at[me, d], beside, os.at[1], orr.at[1])
+    here = [
+        pltpu.make_async_copy(w_ref.at[me], moved.at[me], loc.at[0]),
+        pltpu.make_async_copy(eg_ref, w_gate, loc.at[1]),
+        pltpu.make_async_copy(eu_ref, w_up, loc.at[2]),
+        pltpu.make_async_copy(ed_ref, w_down, loc.at[3]),
+    ]
+    for j in range(1, experts):
+        weight_send(j).start()
+    own.start()
+    own_gates.start()
+    for j in range(1, experts):
+        gate_send(j).start()
+    for c in here:
+        c.start()
+    every[me, d] = x_ref[...]
+    gates[me, d] = g_ref[...]
+    for j in range(1, experts):
+        weight_send(j).wait_recv()
+        weight_twin(j, rows).start()
+        token_send(j).start()
+    for j in range(1, experts):
+        gate_send(j).wait_recv()
+        gate_beside(j, d).start()
+    for c in here:
+        c.wait()
+    own.wait()
+    own_gates.wait()
+
+    def by_beside(j):
+        return send(sums.at[j, 1 - d], from_beside.at[j], beside, ds.at[j], dr.at[j])
+
+    def by_across(j):
+        return send(sums.at[j, d, 1 - t], from_across.at[j], across, xs.at[j], xr.at[j])
+
+    def by_expert(j):
+        return send(
+            zsend.at[j - 1], zrecv.at[j - 1], {"expert": source(j)}, zs.at[j - 1], zr.at[j - 1]
+        )
+
+    def fetch(j):
+        token_send(j).wait_recv()
+        token_across(j, mine).start()
+        token_beside(j, d, mine, 0).start()
+
+    def gather(j):
+        token_across(j, theirs).wait_recv()
+        token_beside(j, d, theirs, 1).start()
+        token_beside(j, 1 - d, mine, 0).wait_recv()
+        token_beside(j, 1 - d, theirs, 1).wait_recv()
+
+    def compute(j):
+        e = source(j)
+        both_rows = 2 * tok_rows
+        x = every[e].reshape(both_rows, features)
+        lanes = gates[e].reshape(both_rows, -1).astype(f32)
+        column = lax.broadcasted_iota(jnp.int32, lanes.shape, 1)
+        gate = jnp.sum(jnp.where(column == me, lanes, 0.0), axis=1, keepdims=True)
+        g = lax.dot_general(x, w_gate[0], ROWS, preferred_element_type=f32)
+        u = lax.dot_general(x, w_up[0], ROWS, preferred_element_type=f32)
+        routed = (g / (1.0 + jnp.exp(-g)) * u * gate).astype(jnp.bfloat16)
+        both = jnp.zeros((both_rows, 2 * share), f32)
+        for i in range(experts):
+            both += lax.dot_general(
+                x[:, i * cut : (i + 1) * cut],
+                moved[i, : 2 * share],
+                ROWS,
+                preferred_element_type=f32,
+            )
+        g, u = both[:, :share], both[:, share:]
+        dense = (g / (1.0 + jnp.exp(-g)) * u).astype(jnp.bfloat16)
+        for i in range(experts):
+            s = jnp.dot(
+                routed, w_down[0, :, i * cut : (i + 1) * cut], preferred_element_type=f32
+            )
+            s += jnp.dot(dense, moved[i, 2 * share :], preferred_element_type=f32)
+            at = (i % per_half) * cut
+            sums[j, :, i // per_half, :, at : at + cut] = s.astype(jnp.bfloat16).reshape(
+                2, tok_rows, cut
+            )
+        by_beside(j).start()
+
+    def join_pair(j):
+        by_beside(j).wait_recv()
+        total = sums[j, d].astype(f32) + from_beside[j].astype(f32)
+        sums[j, d] = total.astype(jnp.bfloat16)
+        by_across(j).start()
+
+    def join_tensor(j):
+        by_across(j).wait_recv()
+        total = sums[j, d, t].astype(f32) + from_across[j].astype(f32)
+        zsend[j - 1] = total.astype(jnp.bfloat16)
+        by_expert(j).start()
+
+    def turn(j, carry):
+        @pl.when(j >= 1)
+        def _():
+            gather(j)
+
+        @pl.when((j >= 1) & (j + 1 < experts))
+        def _():
+            fetch(j + 1)
+
+        compute(j)
+
+        @pl.when(j >= 2)
+        def _():
+            join_tensor(j - 1)
+
+        join_pair(j)
+        return carry
+
+    fetch(1)
+    for j in range(1, experts):
+        weight_twin(j, other_rows).wait_recv()
+        gate_beside(j, 1 - d).wait_recv()
+    lax.fori_loop(0, experts, turn, 0)
+    last = experts - 1
+    join_tensor(last)
+    by_across(0).wait_recv()
+    total = sums[0, d, t].astype(f32) + from_across[0].astype(f32)
+    total += tok_ref[:, mine].astype(f32)
+    for j in range(1, experts):
+        by_expert(j).wait_recv()
+        total += zrecv[j - 1].astype(f32)
+    out_ref[...] = total.astype(out_ref.dtype)
+    for j in range(experts):
+        by_beside(j).wait_send()
+        by_across(j).wait_send()
+    for j in range(1, experts):
+        by_expert(j).wait_send()
+        weight_twin(j, rows).wait_send()
+        gate_send(j).wait_send()
+        weight_send(j).wait_send()
+        gate_beside(j, d).wait_send()
+        token_send(j).wait_send()
+        token_across(j, mine).wait_send()
+        token_beside(j, d, mine, 0).wait_send()
+        token_beside(j, d, theirs, 1).wait_send()
+
+
+def layer(experts, tokens, x, gates, weights, w_gate, w_up, w_down):
+    tok_rows, features = tokens.shape
+    width = features // 2
+    dma = pltpu.SemaphoreType.DMA
+    inside = pl.BlockSpec(memory_space=pltpu.VMEM)
+    anywhere = pl.BlockSpec(memory_space=pl.ANY)
+    kind = tokens.dtype
+    return pl.pallas_call(
+        functools.partial(layer_kernel, experts),
+        out_shape=jax.ShapeDtypeStruct((tok_rows, width), kind),
+        in_specs=[inside] * 3 + [anywhere] * 4,
+        out_specs=inside,
+        scratch_shapes=[
+            pltpu.VMEM((experts, 2) + x.shape, kind),
+            pltpu.VMEM((experts, 2) + gates.shape, kind),
+            pltpu.VMEM(weights.shape, kind),
+            pltpu.VMEM(w_gate.shape, kind),
+            pltpu.VMEM(w_up.shape, kind),
+            pltpu.VMEM(w_down.shape, kind),
+            pltpu.VMEM((experts, 2, 2, tok_rows, width), kind),
+            pltpu.VMEM((experts, 2, tok_rows, width), kind),
+            pltpu.VMEM((experts, tok_rows, width), kind),
+            pltpu.VMEM((experts - 1, tok_rows, width), kind),
+            pltpu.VMEM((experts - 1, tok_rows, width), kind),
+            dma((4,)),
+        ]
+        + [dma((experts,))] * 10
+        + [dma((3, experts))] * 2
+        + [dma((2,))] * 2
+        + [dma((experts,))] * 6,
+        compiler_params=pltpu.CompilerParams(
+            collective_id=0, has_side_effects=True, vmem_limit_bytes=56 * 1024 * 1024
+        ),
+        cost_estimate=pl.CostEstimate(
+            flops=17000000000, bytes_accessed=30000000, transcendentals=1000000
+        ),
+    )(tokens, x, gates, weights, w_gate, w_up, w_down)
+
+
+def local_kernels(
+    tokens,
+    norm_gain,
+    routes,
+    gate_values,
+    dense_gate,
+    dense_up,
+    dense_down,
+    expert_gate,
+    expert_up,
+    expert_down,
+):
+    experts = lax.axis_size("expert")
+    hidden, cut = dense_gate.shape
+    share = -(-hidden // (32 * experts)) * 32
+
+    weights = jnp.stack([dense_gate, dense_up, dense_down])
+    weights = jnp.pad(weights, ((0, 0), (0, share * experts - hidden), (0, 0)))
+    weights = weights.reshape(3, experts, share, cut).transpose(1, 0, 2, 3)
+    weights = weights.reshape(experts, 3 * share, cut)
+    normed = root_normed(tokens, norm_gain)
+    own_gates = jnp.sum(
+        jnp.where(
+            routes[:, :, None] == jnp.arange(128, dtype=jnp.int32),
+            gate_values.astype(jnp.float32)[:, :, None],
+            0.0,
+        ),
+        axis=1,
+    ).astype(jnp.bfloat16)
+    return layer(
+        experts, tokens, normed, own_gates, weights, expert_gate, expert_up, expert_down
+    )
+
+
 def solution(mesh):
     placed = (
         P(("group", "expert", "dp"), None),
@@ -90,8 +387,10 @@
         P("expert", ("tensor", "dp"), None),
         P("expert", ("tensor", "dp"), None),
     )
+    sizes = dict(mesh.shape)
+    paired = sizes["group"] == 2 and sizes["tensor"] == 2 and sizes["dp"] == 2 and sizes["expert"] >= 3
     return jax.shard_map(
-        local,
+        local_kernels if paired else local_plain,
         mesh=mesh,
         in_specs=placed,
         out_specs=P(("group", "expert", "dp"), "tensor"),

time: 356 us -> 172 us (0.48)
  waiting for transfers between devices: 198 us -> 0 us
  Pallas kernels: 0 us -> 163 us
  blocking collectives: 59.6 us -> 0 us
  matrix products: 47.4 us -> 0 us
  local copies, waits for them, and re-layouts: 24.7 us -> 3.85 us
  between operations: 13.3 us -> 0.06 us
  starting transfers between devices: 3.97 us -> 0 us
    pallas_call x0 -> x1, Pallas kernels: none -> 163 us  [layer(): pl.pallas_call(functools.partial(layer_kernel, experts), out_shape=jax.Sh...]
    reduce_scatter x2 -> x0, waiting for transfers between devices: 109 us -> none  [the longest x1 67.6 us: local(): lax.psum_scatter(arranged, ('tensor', 'dp'), scatter_dimension=0, tiled=T...]
    all_gather x2 -> x0, waiting for transfers between devices: 74.9 us -> none  [the longest x1 74.9 us: local(): every = lax.all_gather(normed, 'expert', axis=0, tiled=False)]
    all_gather x1 -> x0, blocking collectives: 59.6 us -> none  [local(): gates = lax.all_gather(own_gates, ('expert', 'dp'), axis=0, tiled=True)]
    dot_general x4 -> x0, matrix products: 47.4 us -> none  [the longest x1 19 us: local(): jnp.dot(expert_hidden, expert_down[0], preferred_element_type=jnp.float32)]
    all_to_all x1 -> x0, waiting for transfers between devices: 13.9 us -> none  [local(): lax.all_to_all(stacked, 'expert', split_axis=1, concat_axis=1, tiled=True)]
    reshape x1, local copies, waits for them, and re-layouts: 15.4 us -> 2.01 us  [local_kernels(): weights = weights.reshape(3, experts, share, cut).transpose(1, 0, 2, 3)]
    transpose x1 -> x0, local copies, waits for them, and re-layouts: 7.41 us -> none  [local(): arranged = combined.astype(jnp.bfloat16).reshape(experts, pairs, tok_rows...]
  transfers between devices with their start and end apart: 5 -> 0, of which waited for: 4 -> 0; matrix products, arithmetic and copies ran while one was open for 1% -> 0% of each run, Pallas kernels for 0% -> 0%
where the time goes in v3:
time: 172 us
  Pallas kernels  163 us (95%)
  other arithmetic  5.13 us (3%)
  local copies, waits for them, and re-layouts  3.85 us (2%)
    pallas_call x1, Pallas kernels, layer(): pl.pallas_call(functools.partial(layer_kernel, experts), out_shape=jax.Sh...  163 us

profile of v3, /device:TPU:0, one launch (start us, length us, event | category | flops | bytes accessed | tf_op | source)
XLA Modules:
  0.0 172.2 jit_solution(5372961523357499238)
XLA Ops:
  0.0 2.9 %fusion.4 = bf16[3,640,896]{2,1,0:T(8,128)(2,1)S(1)} fusion(bf16[1,608,896]{2,1,0:T(8,128)(2,1)} %bitcast.9, bf16[1,608,896]{2,1,0:T(8,128)(2,1)} %bitcast.10, bf16[1,608,896]{2,1,0:T(8,128)(2,1)} %bitcast.11), kind=kLoop, calls=%fused_computation.5 | loop fusion | flops 17203200 | bytes 6709248 | tf_op jit(solution)/shard_map/stack | solution.py:359
  2.9 0.0 copy-start
  2.9 0.0 copy-start.1
  2.9 0.0 copy-start.3
  2.9 0.0 copy-start.2
  2.9 2.0 %copy.14 = bf16[3,4,160,896]{3,2,0,1:T(8,128)(2,1)} copy(bf16[3,4,160,896]{3,2,1,0:T(8,128)(2,1)S(1)} %bitcast.7) | data formatting | bytes 6881280 | tf_op jit(solution)/shard_map/reshape | solution.py:361
  4.9 0.0 copy-done
  4.9 0.3 fusion.5
  5.2 0.0 copy-done.1
  5.2 1.2 fusion.7.x_ref
  6.5 0.0 copy-done.3
  6.5 0.0 copy-done.2
  6.5 0.8 select_reduce_fusion.g_ref
  7.2 163.2 %shard_map.100 = bf16[128,1792]{1,0:T(8,128)(2,1)} custom-call(bf16[128,3584]{1,0:T(8,128)(2,1)} %tok_ref.1, bf16[128,3584]{1,0:T(8,128)(2,1)} %fusion.7.x_ref, bf16[128,128]{1,0:T(8,128)(2,1)} %select_reduce_fusion.g_ref, bf16[4,480,896]{2,1,0:T(8,128)(2,1)} %bitcast.8, bf16[1,608,3584]{2,1,0:T(8,128)(2,1)} %eg_ref.1, bf16[1,608,3584]{2,1,0:T(8,128)(2,1)} %eu_ref.1, ...), custom_call_target="tpu_custom_call" | custom-call | flops 16999999488 | bytes 30000000 | tf_op jit(solution)/shard_map/pallas_call | solution.py:311
  170.4 1.8 %copy.16 = bf16[128,1792]{1,0:T(8,128)(2,1)} copy(bf16[128,1792]{1,0:T(8,128)(2,1)} %shard_map.100) | data formatting | bytes 917504
  (2 shorter events, 0.0 us)
Async XLA Ops:
  2.9 2.1 %copy-start = (bf16[128,3584]{1,0:T(8,128)(2,1)S(1)}, bf16[128,3584]{1,0:T(8,128)(2,1)}, u32[]{:S(2)}) copy-start(bf16[128,3584]{1,0:T(8,128)(2,1)} %tok_ref.1) | copy-start | bytes 2752516
  2.9 2.3 %copy-start.1 = (f32[3584]{0:T(1024)S(1)}, f32[3584]{0:T(1024)}, u32[]{:S(2)}) copy-start(f32[3584]{0:T(1024)} %param.11) | copy-start | bytes 43012
  2.9 3.6 %copy-start.3 = (bf16[128,2]{0,1:T(2,128)(2,1)S(1)}, bf16[128,2]{0,1:T(2,128)(2,1)}, u32[]{:S(2)}) copy-start(bf16[128,2]{0,1:T(2,128)(2,1)} %param.13) | copy-start | bytes 1540
  2.9 3.6 %copy-start.2 = (s32[128,2]{0,1:T(2,128)S(1)}, s32[128,2]{0,1:T(2,128)}, u32[]{:S(2)}) copy-start(s32[128,2]{0,1:T(2,128)} %param.12) | copy-start | bytes 3076
